TPU v7x, 256 devices: a whole 4x4x8 slice. The times are simulated.
256 devices in a mesh: row: 16 (over z_hi, y), col: 16 (over x, z_lo, core).
Axes of the slice: x: 4, y: 4, z: 8 (z_hi: 4, z_lo: 2; z = z_hi * 2 + z_lo), core: 2. Of those that a mesh axis runs over, the one named last changes fastest.
Arguments:
- opening_old: float32 [2048, 2048], P('row', 'col'), may hold values from 0.5 to 1.5
- pressure_old: float32 [2048, 2048], P('row', 'col'), may hold values from -4 to 4
- injection: float32 [2048, 2048], P('row', 'col'), may hold values from 0 to 2
- front_flags: int32 [16, 1024], P('row', 'col'), may hold values 0 or 1
- self_kernel: float32 [256, 256], replicated, may hold values from -0.375 to 0.375
- source_column: int32 [16, 1024, 4], P('row', 'col'), may hold values from 0 to 15, all different within a row; in each aligned block of 64 rows (0 to 63, 64 to 127, ..., all dimensions but the last counted through in order) at most 32 rows name the same one
- source_tile: int32 [16, 1024, 4], P('row', 'col'), may hold values from 0 to 63
- source_rank: int32 [16, 1024, 4], P('row', 'col'), may hold values from 1 to 16
- left_factor: float32 [16, 1024, 4, 16, 256], P('row', 'col'), may hold values from -1.5 to 1.5
- right_factor: float32 [16, 1024, 4, 16, 256], P('row', 'col'), may hold values from -0.375 to 0.375
Outputs:
- opening_new: float32 [2048, 2048], P('row', 'col')
- pressure_new: float32 [2048, 2048], P('row', 'col')
Inputs may be any that keep to these rules, and one draw needn't show every extreme that they name: `source_column`: the 4 sources of a target tile lie in 4 different column blocks; among the 64 target tiles of one device no column block is named more than 32 times, and that count is reached.
All inputs are finite; a program needn't handle non-finite values. No bound on the sum of `front_flags` on one device may be relied on, other than what follows from the above.
Results may differ from a plain program's by a relative error of at most 0.000076.
Values sent between devices are 32-bit elements; how exact they have to be, the bound alone decides.
A program may use at most 64 MiB of HBM per device.

v0:
```python
import jax
import jax.numpy as jnp
from jax import lax
from jax.sharding import PartitionSpec as P

TSIDE = 16
PASSES = 3
step_size = 0.1
highest_mode = lax.Precision.HIGHEST


def with_halo(array, sides, width):
    for axis, dim in sides:
        devices, length = (lax.axis_size(axis), array.shape[dim])
        up = [(i, (i + 1) % devices) for i in range(devices - 1)]
        down = [(j, i) for i, j in up]
        last = lax.slice_in_dim(array, length - width, length, axis=dim)
        leading = lax.slice_in_dim(array, 0, width, axis=dim)
        before = lax.ppermute(last, axis, up)
        after = lax.ppermute(leading, axis, down)
        array = jnp.concatenate([before, array, after], axis=dim)
    return array


def picard_pass(wide_open, wide_press, start_open, inject_part):
    row_count = wide_open.shape[0] - 2
    col_count = wide_open.shape[1] - 2
    cubed_open = wide_open * wide_open * wide_open

    def offset(array, shift_row, shift_col):
        return array[
            1 + shift_row : 1 + shift_row + row_count, 1 + shift_col : 1 + shift_col + col_count
        ]

    cube_middle = offset(cubed_open, 0, 0)
    press_middle = offset(wide_press, 0, 0)
    accumulated = jnp.zeros_like(cube_middle)
    for shift_row, shift_col in ((1, 0), (-1, 0), (0, 1), (0, -1)):
        conduct = (cube_middle + offset(cubed_open, shift_row, shift_col)) / 24.0
        accumulated = accumulated + conduct * (
            offset(wide_press, shift_row, shift_col) - press_middle
        )
    return start_open + step_size * (accumulated + inject_part)


def to_tiles(field_block):
    row_tiles = field_block.shape[0] // TSIDE
    col_tiles = field_block.shape[1] // TSIDE
    shaped = field_block.reshape(row_tiles, TSIDE, col_tiles, TSIDE).transpose(0, 2, 1, 3)
    return shaped.reshape(row_tiles * col_tiles, TSIDE * TSIDE)


def from_tiles(tile_rows, row_tiles, col_tiles):
    shaped = tile_rows.reshape(row_tiles, col_tiles, TSIDE, TSIDE).transpose(0, 2, 1, 3)
    return shaped.reshape(row_tiles * TSIDE, col_tiles * TSIDE)


def local(
    opening_old,
    pressure_old,
    injection,
    front_flags,
    self_kernel,
    source_column,
    source_tile,
    source_rank,
    left_factor,
    right_factor,
):
    block_rows, block_cols = opening_old.shape
    first = with_halo(jnp.stack([opening_old, pressure_old]), (("row", 1), ("col", 2)), 1)
    wide_press = first[1]
    current = picard_pass(first[0], wide_press, opening_old, injection)
    for passes_done in range(1, PASSES):
        wide_open = with_halo(current, (("row", 0), ("col", 1)), 1)
        current = picard_pass(wide_open, wide_press, opening_old, injection)
    row_tiles = block_rows // TSIDE
    col_tiles = block_cols // TSIDE
    tile_rows = to_tiles(current) * front_flags[0][:, None].astype(jnp.float32)
    opening_new = from_tiles(tile_rows, row_tiles, col_tiles)
    tile_count = tile_rows.shape[0]
    links = source_column.shape[2]
    columns = source_column[0].reshape(-1)
    picks = source_tile[0].reshape(-1)
    band = lax.all_gather(tile_rows, "col", axis=0, tiled=True)
    sources = band[columns * tile_count + picks]
    sources = sources.reshape(tile_count, links, -1)
    rank_keep = (
        jnp.arange(right_factor.shape[3], dtype=jnp.int32)[None, None, :]
        < source_rank[0][:, :, None]
    ).astype(jnp.float32)
    coefficients = (
        jnp.einsum("tkjs,tks->tkj", right_factor[0], sources, precision=highest_mode) * rank_keep
    )
    near_terms = jnp.einsum("tkjs,tkj->ts", left_factor[0], coefficients, precision=highest_mode)
    self_terms = jnp.einsum("su,tu->ts", self_kernel, tile_rows, precision=highest_mode)
    pressure_new = from_tiles(self_terms + near_terms, row_tiles, col_tiles)
    return (opening_new, pressure_new)


def solution(mesh):
    return jax.shard_map(
        local,
        mesh=mesh,
        in_specs=(
            P("row", "col"),
            P("row", "col"),
            P("row", "col"),
            P("row", "col"),
            P(),
            P("row", "col", None),
            P("row", "col", None),
            P("row", "col", None),
            P("row", "col", None, None, None),
            P("row", "col", None, None, None),
        ),
        out_specs=(P("row", "col"), P("row", "col")),
        check_vma=False,
    )
```

profile of v0, /device:TPU:1, one launch (start us, length us, event | category | flops | bytes accessed | tf_op | source)
XLA Modules:
  0.0 133.9 jit_solution(10966128705149386193)
XLA Ops:
  8.0 1.3 collective-permute-start.1
  9.3 4.7 %collective-permute-start = (f32[2,1,128]{2,1,0:T(1,128)S(1)}, f32[2,1,128]{2,1,0:T(1,128)S(1)}, u32[]{:S(2)}, u32[]{:S(2)}) collective-permute-start(f32[2,1,128]{2,1,0:T(1,128)S(1)} %get-tuple-element.6), channel_id=1, source_target_pairs={{0,16},{16,32},{32,48},{48,64},{64,80},{80,96},{96,112},{112,128},... | collective-permute-start | bytes 3080 | tf_op jit(solution)/shard_map/ppermute | solution.py:19
  14.7 0.9 pad_maximum_fusion.1
  15.7 5.6 %collective-permute-start.3 = (f32[2,130,1]{2,1,0:T(8,128)S(1)}, f32[2,130,1]{2,1,0:T(8,128)S(1)}, u32[]{:S(2)}, u32[]{:S(2)}) collective-permute-start(f32[2,130,1]{2,1,0:T(8,128)S(1)} %get-tuple-element.5), channel_id=1, source_target_pairs={{1,0},{2,1},{3,2},{4,3},{5,4},{6,5},{7,6},{8,7},{9,8},{10,9},{11,1... | collective-permute-start | bytes 3128 | tf_op jit(solution)/shard_map/ppermute | solution.py:20
  21.3 1.9 %collective-permute-start.2 = (f32[2,130,1]{2,1,0:T(8,128)S(1)}, f32[2,130,1]{2,1,0:T(8,128)S(1)}, u32[]{:S(2)}, u32[]{:S(2)}) collective-permute-start(f32[2,130,1]{2,1,0:T(8,128)S(1)} %get-tuple-element.4), channel_id=1, source_target_pairs={{0,1},{1,2},{2,3},{3,4},{4,5},{5,6},{6,7},{7,8},{8,9},{9,10},{10,1... | collective-permute-start | bytes 3128 | tf_op jit(solution)/shard_map/ppermute | solution.py:19
  23.8 1.4 %collective-permute-done.2 = f32[2,130,1]{2,1,0:T(8,128)S(1)} collective-permute-done((f32[2,130,1]{2,1,0:T(8,128)S(1)}, f32[2,130,1]{2,1,0:T(8,128)S(1)}, u32[]{:S(2)}, u32[]{:S(2)}) %collective-permute-start.2) | collective-permute-done | bytes 1072 | tf_op jit(solution)/shard_map/ppermute | solution.py:19
  25.2 1.1 pad_maximum_fusion
  26.4 1.1 fusion.38
  27.5 1.3 collective-permute-start.5
  28.8 4.5 %collective-permute-start.4 = (f32[1,128]{1,0:T(1,128)S(1)}, f32[1,128]{1,0:T(1,128)S(1)}, u32[]{:S(2)}, u32[]{:S(2)}) collective-permute-start(f32[1,128]{1,0:T(1,128)S(1)} %get-tuple-element.14), channel_id=1, source_target_pairs={{0,16},{16,32},{32,48},{48,64},{64,80},{80,96},{96,112},{112,128},... | collective-permute-start | bytes 1544 | tf_op jit(solution)/shard_map/ppermute | solution.py:19
  34.1 2.2 %collective-permute-start.7 = (f32[130,1]{1,0:T(8,128)S(1)}, f32[130,1]{1,0:T(8,128)S(1)}, u32[]{:S(2)}, u32[]{:S(2)}) collective-permute-start(f32[130,1]{1,0:T(8,128)S(1)} %get-tuple-element.11), channel_id=1, source_target_pairs={{1,0},{2,1},{3,2},{4,3},{5,4},{6,5},{7,6},{8,7},{9,8},{10,9},{11,1... | collective-permute-start | bytes 1568 | tf_op jit(solution)/shard_map/ppermute | solution.py:20
  36.3 4.9 %collective-permute-start.6 = (f32[130,1]{1,0:T(8,128)S(1)}, f32[130,1]{1,0:T(8,128)S(1)}, u32[]{:S(2)}, u32[]{:S(2)}) collective-permute-start(f32[130,1]{1,0:T(8,128)S(1)} %get-tuple-element.10), channel_id=1, source_target_pairs={{0,1},{1,2},{2,3},{3,4},{4,5},{5,6},{6,7},{7,8},{8,9},{9,10},{10,1... | collective-permute-start | bytes 1568 | tf_op jit(solution)/shard_map/ppermute | solution.py:19
  41.3 1.3 collective-permute-done.6
  42.7 1.1 fusion.24
  43.8 1.3 collective-permute-start.9
  45.1 4.5 %collective-permute-start.8 = (f32[1,128]{1,0:T(1,128)S(1)}, f32[1,128]{1,0:T(1,128)S(1)}, u32[]{:S(2)}, u32[]{:S(2)}) collective-permute-start(f32[1,128]{1,0:T(1,128)S(1)} %get-tuple-element.12), channel_id=1, source_target_pairs={{0,16},{16,32},{32,48},{48,64},{64,80},{80,96},{96,112},{112,128},... | collective-permute-start | bytes 1544 | tf_op jit(solution)/shard_map/ppermute | solution.py:19
  50.5 1.9 %collective-permute-start.11 = (f32[130,1]{1,0:T(8,128)S(1)}, f32[130,1]{1,0:T(8,128)S(1)}, u32[]{:S(2)}, u32[]{:S(2)}) collective-permute-start(f32[130,1]{1,0:T(8,128)S(1)} %get-tuple-element.9), channel_id=1, source_target_pairs={{1,0},{2,1},{3,2},{4,3},{5,4},{6,5},{7,6},{8,7},{9,8},{10,9},{11,1... | collective-permute-start | bytes 1568 | tf_op jit(solution)/shard_map/ppermute | solution.py:20
  52.4 5.1 %collective-permute-start.10 = (f32[130,1]{1,0:T(8,128)S(1)}, f32[130,1]{1,0:T(8,128)S(1)}, u32[]{:S(2)}, u32[]{:S(2)}) collective-permute-start(f32[130,1]{1,0:T(8,128)S(1)} %get-tuple-element.8), channel_id=1, source_target_pairs={{0,1},{1,2},{2,3},{3,4},{4,5},{5,6},{6,7},{7,8},{8,9},{9,10},{10,1... | collective-permute-start | bytes 1568 | tf_op jit(solution)/shard_map/ppermute | solution.py:19
  57.9 0.9 collective-permute-done.10
  59.0 0.8 fusion.47
  61.5 53.2 %all-gather.2.cloned.1.call-done = f32[1024,256]{1,0:T(8,128)} async-done(((f32[64,256]{1,0:T(8,128)}), f32[1024,256]{1,0:T(8,128)}) %all-gather.2.cloned.1.call-update) | async-done | bytes 1048592 | tf_op jit(solution)/shard_map/all_gather | solution.py:85
  114.7 2.2 %gather_fusion = f32[256,256]{1,0:T(8,128)S(1)} fusion(f32[1024,256]{1,0:T(8,128)} %all-gather.2.cloned.1.call-done, s32[1024]{0:T(1024)S(1)} %pad_clamp_fusion), kind=kCustom, calls=%fused_computation | custom fusion | bytes 525312 | tf_op jit(solution)/shard_map/gather | solution.py:86
  117.1 5.9 %fusion.2 = f32[64,4,1,16]{3,2,1,0:T(1,128)S(1)} fusion(f32[64,4,256,1]{2,3,1,0:T(1,128)S(1)} %reshape.88, f32[1,64,4,16,256]{4,3,2,1,0:T(8,128)} %param.19), kind=kOutput, calls=%fused_computation.3 | convolution fusion | flops 12582912 | bytes 4472832 | tf_op jit(solution)/shard_map/tkjs,tks->tkj/dot_general | solution.py:93
  123.2 2.4 %fusion = f32[64,1,256,1]{2,1,3,0:T(1,128)S(1)} fusion(f32[64,4,16,1]{2,3,1,0:T(1,128)S(1)} %bitcast.48, f32[1,64,4,16,256]{4,3,2,1,0:T(8,128)S(1)} %copy-done.1), kind=kOutput, calls=%fused_computation.1 | convolution fusion | flops 12582912 | bytes 4276224 | tf_op jit(solution)/shard_map/tkjs,tkj->ts/dot_general | solution.py:95
  (62 shorter events, 8.0 us)
Async XLA Ops:
  7.2 118.4 %copy-start = (f32[256,256]{1,0:T(8,128)S(1)}, f32[256,256]{1,0:T(8,128)}, u32[]{:S(2)}) copy-start(f32[256,256]{1,0:T(8,128)} %param.14) | copy-start | bytes 786436
  7.2 51.8 %copy-start.2 = (f32[128,128]{1,0:T(8,128)S(1)}, f32[128,128]{1,0:T(8,128)}, u32[]{:S(2)}) copy-start(f32[128,128]{1,0:T(8,128)} %param.10) | copy-start | bytes 196612
  7.2 51.8 %copy-start.4 = (f32[128,128]{1,0:T(8,128)S(1)}, f32[128,128]{1,0:T(8,128)}, u32[]{:S(2)}) copy-start(f32[128,128]{1,0:T(8,128)} %param.12) | copy-start | bytes 196612
  7.2 42.5 %copy-start.8 = (s32[1,64]{1,0:T(1,128)S(1)}, s32[1,64]{1,0:T(1,128)}, u32[]{:S(2)}) copy-start(s32[1,64]{1,0:T(1,128)} %param.13) | copy-start | bytes 772
  7.2 107.4 %all-gather.2.cloned.1.call-start = ((), (), s32[]{:S(2)}) async-start(), calls=%async_computation | async-start | bytes 1114112 | tf_op jit(solution)/shard_map/all_gather | solution.py:85
  8.0 6.0 %collective-permute-start.1 = (f32[2,1,128]{2,1,0:T(1,128)S(1)}, f32[2,1,128]{2,1,0:T(1,128)S(1)}, u32[]{:S(2)}, u32[]{:S(2)}) collective-permute-start(f32[2,1,128]{2,1,0:T(1,128)S(1)} %get-tuple-element.7), channel_id=1, source_target_pairs={{16,0},{32,16},{48,32},{64,48},{80,64},{96,80},{112,96},{128,112},... | collective-permute-start | bytes 3080 | tf_op jit(solution)/shard_map/ppermute | solution.py:20
  9.3 5.4 %collective-permute-start = (f32[2,1,128]{2,1,0:T(1,128)S(1)}, f32[2,1,128]{2,1,0:T(1,128)S(1)}, u32[]{:S(2)}, u32[]{:S(2)}) collective-permute-start(f32[2,1,128]{2,1,0:T(1,128)S(1)} %get-tuple-element.6), channel_id=1, source_target_pairs={{0,16},{16,32},{32,48},{48,64},{64,80},{80,96},{96,112},{112,128},... | collective-permute-start | bytes 3080 | tf_op jit(solution)/shard_map/ppermute | solution.py:19
  15.7 8.1 %collective-permute-start.3 = (f32[2,130,1]{2,1,0:T(8,128)S(1)}, f32[2,130,1]{2,1,0:T(8,128)S(1)}, u32[]{:S(2)}, u32[]{:S(2)}) collective-permute-start(f32[2,130,1]{2,1,0:T(8,128)S(1)} %get-tuple-element.5), channel_id=1, source_target_pairs={{1,0},{2,1},{3,2},{4,3},{5,4},{6,5},{7,6},{8,7},{9,8},{10,9},{11,1... | collective-permute-start | bytes 3128 | tf_op jit(solution)/shard_map/ppermute | solution.py:20
  21.3 3.9 %collective-permute-start.2 = (f32[2,130,1]{2,1,0:T(8,128)S(1)}, f32[2,130,1]{2,1,0:T(8,128)S(1)}, u32[]{:S(2)}, u32[]{:S(2)}) collective-permute-start(f32[2,130,1]{2,1,0:T(8,128)S(1)} %get-tuple-element.4), channel_id=1, source_target_pairs={{0,1},{1,2},{2,3},{3,4},{4,5},{5,6},{6,7},{7,8},{8,9},{9,10},{10,1... | collective-permute-start | bytes 3128 | tf_op jit(solution)/shard_map/ppermute | solution.py:19
  26.3 34.8 %copy-start.5 = (s32[1,64,4]{1,2,0:T(4,128)S(1)}, s32[1,64,4]{1,2,0:T(4,128)}, u32[]{:S(2)}) copy-start(s32[1,64,4]{1,2,0:T(4,128)} %param.16) | copy-start | bytes 3076
  26.3 34.8 %copy-start.6 = (s32[1,64,4]{1,2,0:T(4,128)S(1)}, s32[1,64,4]{1,2,0:T(4,128)}, u32[]{:S(2)}) copy-start(s32[1,64,4]{1,2,0:T(4,128)} %param.15) | copy-start | bytes 3076
  26.3 35.0 %copy-start.7 = (s32[1,64,4]{1,2,0:T(4,128)S(1)}, s32[1,64,4]{1,2,0:T(4,128)}, u32[]{:S(2)}) copy-start(s32[1,64,4]{1,2,0:T(4,128)} %param.17) | copy-start | bytes 3076
  27.5 5.8 %collective-permute-start.5 = (f32[1,128]{1,0:T(1,128)S(1)}, f32[1,128]{1,0:T(1,128)S(1)}, u32[]{:S(2)}, u32[]{:S(2)}) collective-permute-start(f32[1,128]{1,0:T(1,128)S(1)} %get-tuple-element.15), channel_id=1, source_target_pairs={{16,0},{32,16},{48,32},{64,48},{80,64},{96,80},{112,96},{128,112},... | collective-permute-start | bytes 1544 | tf_op jit(solution)/shard_map/ppermute | solution.py:20
  28.8 5.2 %collective-permute-start.4 = (f32[1,128]{1,0:T(1,128)S(1)}, f32[1,128]{1,0:T(1,128)S(1)}, u32[]{:S(2)}, u32[]{:S(2)}) collective-permute-start(f32[1,128]{1,0:T(1,128)S(1)} %get-tuple-element.14), channel_id=1, source_target_pairs={{0,16},{16,32},{32,48},{48,64},{64,80},{80,96},{96,112},{112,128},... | collective-permute-start | bytes 1544 | tf_op jit(solution)/shard_map/ppermute | solution.py:19
  34.1 7.2 %collective-permute-start.7 = (f32[130,1]{1,0:T(8,128)S(1)}, f32[130,1]{1,0:T(8,128)S(1)}, u32[]{:S(2)}, u32[]{:S(2)}) collective-permute-start(f32[130,1]{1,0:T(8,128)S(1)} %get-tuple-element.11), channel_id=1, source_target_pairs={{1,0},{2,1},{3,2},{4,3},{5,4},{6,5},{7,6},{8,7},{9,8},{10,9},{11,1... | collective-permute-start | bytes 1568 | tf_op jit(solution)/shard_map/ppermute | solution.py:20
  36.3 6.3 %collective-permute-start.6 = (f32[130,1]{1,0:T(8,128)S(1)}, f32[130,1]{1,0:T(8,128)S(1)}, u32[]{:S(2)}, u32[]{:S(2)}) collective-permute-start(f32[130,1]{1,0:T(8,128)S(1)} %get-tuple-element.10), channel_id=1, source_target_pairs={{0,1},{1,2},{2,3},{3,4},{4,5},{5,6},{6,7},{7,8},{8,9},{9,10},{10,1... | collective-permute-start | bytes 1568 | tf_op jit(solution)/shard_map/ppermute | solution.py:19
  43.8 5.8 %collective-permute-start.9 = (f32[1,128]{1,0:T(1,128)S(1)}, f32[1,128]{1,0:T(1,128)S(1)}, u32[]{:S(2)}, u32[]{:S(2)}) collective-permute-start(f32[1,128]{1,0:T(1,128)S(1)} %get-tuple-element.13), channel_id=1, source_target_pairs={{16,0},{32,16},{48,32},{64,48},{80,64},{96,80},{112,96},{128,112},... | collective-permute-start | bytes 1544 | tf_op jit(solution)/shard_map/ppermute | solution.py:20
  45.1 5.2 %collective-permute-start.8 = (f32[1,128]{1,0:T(1,128)S(1)}, f32[1,128]{1,0:T(1,128)S(1)}, u32[]{:S(2)}, u32[]{:S(2)}) collective-permute-start(f32[1,128]{1,0:T(1,128)S(1)} %get-tuple-element.12), channel_id=1, source_target_pairs={{0,16},{16,32},{32,48},{48,64},{64,80},{80,96},{96,112},{112,128},... | collective-permute-start | bytes 1544 | tf_op jit(solution)/shard_map/ppermute | solution.py:19
  50.5 7.5 %collective-permute-start.11 = (f32[130,1]{1,0:T(8,128)S(1)}, f32[130,1]{1,0:T(8,128)S(1)}, u32[]{:S(2)}, u32[]{:S(2)}) collective-permute-start(f32[130,1]{1,0:T(8,128)S(1)} %get-tuple-element.9), channel_id=1, source_target_pairs={{1,0},{2,1},{3,2},{4,3},{5,4},{6,5},{7,6},{8,7},{9,8},{10,9},{11,1... | collective-permute-start | bytes 1568 | tf_op jit(solution)/shard_map/ppermute | solution.py:20
  52.4 6.5 %collective-permute-start.10 = (f32[130,1]{1,0:T(8,128)S(1)}, f32[130,1]{1,0:T(8,128)S(1)}, u32[]{:S(2)}, u32[]{:S(2)}) collective-permute-start(f32[130,1]{1,0:T(8,128)S(1)} %get-tuple-element.8), channel_id=1, source_target_pairs={{0,1},{1,2},{2,3},{3,4},{4,5},{5,6},{6,7},{7,8},{8,9},{9,10},{10,1... | collective-permute-start | bytes 1568 | tf_op jit(solution)/shard_map/ppermute | solution.py:19
  117.1 6.0 %copy-start.1 = (f32[1,64,4,16,256]{4,3,2,1,0:T(8,128)S(1)}, f32[1,64,4,16,256]{4,3,2,1,0:T(8,128)}, u32[]{:S(2)}) copy-start(f32[1,64,4,16,256]{4,3,2,1,0:T(8,128)} %param.18) | copy-start | bytes 12582916
  117.1 8.4 %copy-start.3 = (f32[64,256]{1,0:T(8,128)S(1)}, f32[64,256]{1,0:T(8,128)}, u32[]{:S(2)}) copy-start(f32[64,256]{1,0:T(8,128)} %broadcast_multiply_fusion) | copy-start | bytes 196612
Sparse Core Ops, SparseCore 0:
  61.2 53.3 all-gather.1
where the time goes:
time: 135 us; the launch traced here: 134 us
  waiting for transfers between devices  59.5 us (44%)
  starting transfers between devices  39.3 us (29%)
  between operations  14.5 us (11%)
  matrix products  8.59 us (6%)
  other arithmetic  6.9 us (5%)
  local copies, waits for them, and re-layouts  5.14 us (4%)
    all_gather x1, waiting for transfers between devices, local(): band = lax.all_gather(tile_rows, 'col', axis=0, tiled=True)  53.2 us
    ppermute x6, starting transfers between devices, with_halo(): before = lax.ppermute(last, axis, up)  25.6 us
    ppermute x6, starting transfers between devices, with_halo(): after = lax.ppermute(leading, axis, down)  13.6 us
    dot_general x1, matrix products, local(): jnp.einsum('tkjs,tks->tkj', right_factor[0], sources, precision=highest_m...  5.86 us
    ppermute x6, waiting for transfers between devices, with_halo(): before = lax.ppermute(last, axis, up)  5.71 us
  transfers between devices with their start and end apart: 13, of which 8 were waited for; matrix products, arithmetic and copies ran while one was open for 1% of the time, Pallas kernels for 0%

commit v1 on v0

--- a/solution.py
+++ b/solution.py
@@ -82,7 +82,9 @@
     links = source_column.shape[2]
     columns = source_column[0].reshape(-1)
     picks = source_tile[0].reshape(-1)
-    band = lax.all_gather(tile_rows, "col", axis=0, tiled=True)
+    band = jnp.concatenate(
+        lax.all_to_all(jnp.stack([tile_rows] * lax.axis_size("col")), "col", 0, 0), axis=0
+    )
     sources = band[columns * tile_count + picks]
     sources = sources.reshape(tile_count, links, -1)
     rank_keep = (

time: 135 us -> 105 us (0.78)
  the two profiles are of different devices: /device:TPU:1 before, /device:TPU:128 now
where the time goes in v1:
time: 105 us; the launch traced here: 104 us
  starting transfers between devices  45.3 us (43%)
  waiting for transfers between devices  37.7 us (36%)
  matrix products  8.59 us (8%)
  other arithmetic  6.29 us (6%)
  local copies, waits for them, and re-layouts  5.04 us (5%)
  between operations  1.08 us (1%)
    ppermute x6, starting transfers between devices, with_halo(): before = lax.ppermute(last, axis, up)  22.1 us
    ppermute x6, waiting for transfers between devices, with_halo(): before = lax.ppermute(last, axis, up)  21.5 us
    all_to_all x1, waiting for transfers between devices, local(): lax.all_to_all(jnp.stack([tile_rows] * lax.axis_size('col')), 'col', 0, 0)  16.2 us
    ppermute x6, starting transfers between devices, with_halo(): after = lax.ppermute(leading, axis, down)  11.8 us
    all_to_all x1, starting transfers between devices, local(): lax.all_to_all(jnp.stack([tile_rows] * lax.axis_size('col')), 'col', 0, 0)  11.4 us
    dot_general x1, matrix products, local(): jnp.einsum('tkjs,tks->tkj', right_factor[0], sources, precision=highest_m...  5.86 us
    dot_general x1, matrix products, local(): jnp.einsum('tkjs,tkj->ts', left_factor[0], coefficients, precision=highes...  2.35 us
    add x2, other arithmetic, picard_pass(): return start_open + step_size * (accumulated + inject_part)  2.17 us
  transfers between devices with their start and end apart: 13, of which 7 were waited for; matrix products, arithmetic and copies ran while one was open for 1% of the time, Pallas kernels for 0%

profile of v1, /device:TPU:128, one launch (start us, length us, event | category | flops | bytes accessed | tf_op | source)
XLA Modules:
  0.0 104.0 jit_solution(5427995327345365910)
XLA Ops:
  1.5 4.0 %collective-permute-start.1 = (f32[2,1,128]{2,1,0:T(1,128)S(1)}, f32[2,1,128]{2,1,0:T(1,128)S(1)}, u32[]{:S(2)}, u32[]{:S(2)}) collective-permute-start(f32[2,1,128]{2,1,0:T(1,128)S(1)} %get-tuple-element.7), channel_id=1, source_target_pairs={{16,0},{32,16},{48,32},{64,48},{80,64},{96,80},{112,96},{128,112},... | collective-permute-start | bytes 3080 | tf_op jit(solution)/shard_map/ppermute | solution.py:20
  5.5 1.9 %collective-permute-start = (f32[2,1,128]{2,1,0:T(1,128)S(1)}, f32[2,1,128]{2,1,0:T(1,128)S(1)}, u32[]{:S(2)}, u32[]{:S(2)}) collective-permute-start(f32[2,1,128]{2,1,0:T(1,128)S(1)} %get-tuple-element.6), channel_id=1, source_target_pairs={{0,16},{16,32},{32,48},{48,64},{64,80},{80,96},{96,112},{112,128},... | collective-permute-start | bytes 3080 | tf_op jit(solution)/shard_map/ppermute | solution.py:19
  7.4 7.7 %collective-permute-done = f32[2,1,128]{2,1,0:T(1,128)S(1)} collective-permute-done((f32[2,1,128]{2,1,0:T(1,128)S(1)}, f32[2,1,128]{2,1,0:T(1,128)S(1)}, u32[]{:S(2)}, u32[]{:S(2)}) %collective-permute-start) | collective-permute-done | bytes 1056 | tf_op jit(solution)/shard_map/ppermute | solution.py:19
  16.2 1.3 %collective-permute-start.3 = (f32[2,130,1]{2,1,0:T(8,128)S(1)}, f32[2,130,1]{2,1,0:T(8,128)S(1)}, u32[]{:S(2)}, u32[]{:S(2)}) collective-permute-start(f32[2,130,1]{2,1,0:T(8,128)S(1)} %get-tuple-element.5), channel_id=1, source_target_pairs={{1,0},{2,1},{3,2},{4,3},{5,4},{6,5},{7,6},{8,7},{9,8},{10,9},{11,1... | collective-permute-start | bytes 3128 | tf_op jit(solution)/shard_map/ppermute | solution.py:20
  17.5 3.0 %collective-permute-start.2 = (f32[2,130,1]{2,1,0:T(8,128)S(1)}, f32[2,130,1]{2,1,0:T(8,128)S(1)}, u32[]{:S(2)}, u32[]{:S(2)}) collective-permute-start(f32[2,130,1]{2,1,0:T(8,128)S(1)} %get-tuple-element.4), channel_id=1, source_target_pairs={{0,1},{1,2},{2,3},{3,4},{4,5},{5,6},{6,7},{7,8},{8,9},{9,10},{10,1... | collective-permute-start | bytes 3128 | tf_op jit(solution)/shard_map/ppermute | solution.py:19
  21.5 1.1 %pad_maximum_fusion = f32[2,130,130]{2,1,0:T(8,128)S(1)} fusion(f32[2,130,1]{2,1,0:T(8,128)S(1)} %collective-permute-done.3, f32[2,1,128]{2,1,0:T(1,128)S(1)} %collective-permute-done.1, f32[1,128,128]{2,1,0:T(8,128)} %bitcast.48, f32[1,128,128]{2,1,0:T(8,128)} %bitcast.43, f32[2,1,128]{2,1,0:T(1,128)S(1)} %collective-permute-done, ...), kind=kLoop, calls=%fused_computation.7 | loop fusion | flops 169000 | bytes 270400 | tf_op jit(solution)/shard_map/concatenate | solution.py:21
  22.6 1.1 %fusion.38 = f32[128,128]{1,0:T(8,128)S(1)} fusion(f32[128,128]{1,0:T(8,128)} %param.10, f32[128,128]{1,0:T(8,128)} %param.12, f32[130,130]{1,0:T(8,128)S(1)} %multiply_multiply_fusion.2, f32[130,130]{1,0:T(8,128)S(1)} %slice_bitcast_fusion), kind=kLoop, calls=%fused_computation.61 | loop fusion | flops 360448 | bytes 851968 | tf_op jit(solution)/shard_map/add | solution.py:43
  23.7 1.9 %collective-permute-start.5 = (f32[1,128]{1,0:T(1,128)S(1)}, f32[1,128]{1,0:T(1,128)S(1)}, u32[]{:S(2)}, u32[]{:S(2)}) collective-permute-start(f32[1,128]{1,0:T(1,128)S(1)} %get-tuple-element.15), channel_id=1, source_target_pairs={{16,0},{32,16},{48,32},{64,48},{80,64},{96,80},{112,96},{128,112},... | collective-permute-start | bytes 1544 | tf_op jit(solution)/shard_map/ppermute | solution.py:20
  25.6 3.9 %collective-permute-start.4 = (f32[1,128]{1,0:T(1,128)S(1)}, f32[1,128]{1,0:T(1,128)S(1)}, u32[]{:S(2)}, u32[]{:S(2)}) collective-permute-start(f32[1,128]{1,0:T(1,128)S(1)} %get-tuple-element.14), channel_id=1, source_target_pairs={{0,16},{16,32},{32,48},{48,64},{64,80},{80,96},{96,112},{112,128},... | collective-permute-start | bytes 1544 | tf_op jit(solution)/shard_map/ppermute | solution.py:19
  29.5 5.7 %collective-permute-done.4 = f32[1,128]{1,0:T(1,128)S(1)} collective-permute-done((f32[1,128]{1,0:T(1,128)S(1)}, f32[1,128]{1,0:T(1,128)S(1)}, u32[]{:S(2)}, u32[]{:S(2)}) %collective-permute-start.4) | collective-permute-done | bytes 544 | tf_op jit(solution)/shard_map/ppermute | solution.py:19
  35.4 1.3 %collective-permute-start.7 = (f32[130,1]{1,0:T(8,128)S(1)}, f32[130,1]{1,0:T(8,128)S(1)}, u32[]{:S(2)}, u32[]{:S(2)}) collective-permute-start(f32[130,1]{1,0:T(8,128)S(1)} %get-tuple-element.11), channel_id=1, source_target_pairs={{1,0},{2,1},{3,2},{4,3},{5,4},{6,5},{7,6},{8,7},{9,8},{10,9},{11,1... | collective-permute-start | bytes 1568 | tf_op jit(solution)/shard_map/ppermute | solution.py:20
  36.7 3.9 %collective-permute-start.6 = (f32[130,1]{1,0:T(8,128)S(1)}, f32[130,1]{1,0:T(8,128)S(1)}, u32[]{:S(2)}, u32[]{:S(2)}) collective-permute-start(f32[130,1]{1,0:T(8,128)S(1)} %get-tuple-element.10), channel_id=1, source_target_pairs={{0,1},{1,2},{2,3},{3,4},{4,5},{5,6},{6,7},{7,8},{8,9},{9,10},{10,1... | collective-permute-start | bytes 1568 | tf_op jit(solution)/shard_map/ppermute | solution.py:19
  41.6 1.1 %fusion.24 = f32[128,128]{1,0:T(8,128)S(1)} fusion(f32[128,128]{1,0:T(8,128)} %param.10, f32[128,128]{1,0:T(8,128)} %param.12, f32[130,130]{1,0:T(8,128)S(1)} %multiply_multiply_fusion.1, f32[130,130]{1,0:T(8,128)S(1)} %slice_bitcast_fusion), kind=kLoop, calls=%fused_computation.42 | loop fusion | flops 360448 | bytes 851968 | tf_op jit(solution)/shard_map/add | solution.py:43
  42.7 2.0 %collective-permute-start.9 = (f32[1,128]{1,0:T(1,128)S(1)}, f32[1,128]{1,0:T(1,128)S(1)}, u32[]{:S(2)}, u32[]{:S(2)}) collective-permute-start(f32[1,128]{1,0:T(1,128)S(1)} %get-tuple-element.13), channel_id=1, source_target_pairs={{16,0},{32,16},{48,32},{64,48},{80,64},{96,80},{112,96},{128,112},... | collective-permute-start | bytes 1544 | tf_op jit(solution)/shard_map/ppermute | solution.py:20
  44.7 3.9 %collective-permute-start.8 = (f32[1,128]{1,0:T(1,128)S(1)}, f32[1,128]{1,0:T(1,128)S(1)}, u32[]{:S(2)}, u32[]{:S(2)}) collective-permute-start(f32[1,128]{1,0:T(1,128)S(1)} %get-tuple-element.12), channel_id=1, source_target_pairs={{0,16},{16,32},{32,48},{48,64},{64,80},{80,96},{96,112},{112,128},... | collective-permute-start | bytes 1544 | tf_op jit(solution)/shard_map/ppermute | solution.py:19
  48.6 5.7 %collective-permute-done.8 = f32[1,128]{1,0:T(1,128)S(1)} collective-permute-done((f32[1,128]{1,0:T(1,128)S(1)}, f32[1,128]{1,0:T(1,128)S(1)}, u32[]{:S(2)}, u32[]{:S(2)}) %collective-permute-start.8) | collective-permute-done | bytes 544 | tf_op jit(solution)/shard_map/ppermute | solution.py:19
  54.5 1.3 %collective-permute-start.11 = (f32[130,1]{1,0:T(8,128)S(1)}, f32[130,1]{1,0:T(8,128)S(1)}, u32[]{:S(2)}, u32[]{:S(2)}) collective-permute-start(f32[130,1]{1,0:T(8,128)S(1)} %get-tuple-element.9), channel_id=1, source_target_pairs={{1,0},{2,1},{3,2},{4,3},{5,4},{6,5},{7,6},{8,7},{9,8},{10,9},{11,1... | collective-permute-start | bytes 1568 | tf_op jit(solution)/shard_map/ppermute | solution.py:20
  55.8 5.4 %collective-permute-start.10 = (f32[130,1]{1,0:T(8,128)S(1)}, f32[130,1]{1,0:T(8,128)S(1)}, u32[]{:S(2)}, u32[]{:S(2)}) collective-permute-start(f32[130,1]{1,0:T(8,128)S(1)} %get-tuple-element.8), channel_id=1, source_target_pairs={{0,1},{1,2},{2,3},{3,4},{4,5},{5,6},{6,7},{7,8},{8,9},{9,10},{10,1... | collective-permute-start | bytes 1568 | tf_op jit(solution)/shard_map/ppermute | solution.py:19
  63.7 1.1 %stack.11 = f32[16,64,256]{2,1,0:T(8,128)} broadcast(f32[64,256]{1,0:T(8,128)S(1)} %broadcast_multiply_fusion), dimensions={1,2} | broadcast | bytes 1114112 | tf_op jit(solution)/shard_map/stack | solution.py:86
  64.8 11.4 %all-to-all-start = ((f32[16,64,256]{2,1,0:T(8,128)}), f32[16,64,256]{2,1,0:T(8,128)S(1)}, u32[]{:S(2)}, u32[]{:S(2)}) async-start(f32[16,64,256]{2,1,0:T(8,128)} %stack.11), calls=%async_computation | async-start | bytes 2097152 | tf_op jit(solution)/shard_map/all_to_all | solution.py:86
  76.6 16.2 %all-to-all-done = f32[16,64,256]{2,1,0:T(8,128)S(1)} async-done(((f32[16,64,256]{2,1,0:T(8,128)}), f32[16,64,256]{2,1,0:T(8,128)S(1)}, u32[]{:S(2)}, u32[]{:S(2)}) %all-to-all-start) | async-done | bytes 1048608 | tf_op jit(solution)/shard_map/all_to_all | solution.py:86
  92.8 1.0 gather_fusion
  94.1 5.9 %fusion.2 = f32[64,4,1,16]{3,2,1,0:T(1,128)S(1)} fusion(f32[64,4,256,1]{2,3,1,0:T(1,128)S(1)} %reshape.101, f32[1,64,4,16,256]{4,3,2,1,0:T(8,128)} %param.19), kind=kOutput, calls=%fused_computation.3 | convolution fusion | flops 12582912 | bytes 4472832 | tf_op jit(solution)/shard_map/tkjs,tks->tkj/dot_general | solution.py:95
  100.1 2.4 %fusion = f32[64,1,256,1]{2,1,3,0:T(1,128)S(1)} fusion(f32[64,4,16,1]{2,3,1,0:T(1,128)S(1)} %bitcast.50, f32[1,64,4,16,256]{4,3,2,1,0:T(8,128)S(1)} %copy-done.1), kind=kOutput, calls=%fused_computation.1 | convolution fusion | flops 12582912 | bytes 4276224 | tf_op jit(solution)/shard_map/tkjs,tkj->ts/dot_general | solution.py:97
  (60 shorter events, 8.7 us)
Async XLA Ops:
  0.6 101.8 %copy-start = (f32[256,256]{1,0:T(8,128)S(1)}, f32[256,256]{1,0:T(8,128)}, u32[]{:S(2)}) copy-start(f32[256,256]{1,0:T(8,128)} %param.14) | copy-start | bytes 786436
  0.6 61.6 %copy-start.2 = (f32[128,128]{1,0:T(8,128)S(1)}, f32[128,128]{1,0:T(8,128)}, u32[]{:S(2)}) copy-start(f32[128,128]{1,0:T(8,128)} %param.10) | copy-start | bytes 196612
  0.7 61.6 %copy-start.3 = (f32[128,128]{1,0:T(8,128)S(1)}, f32[128,128]{1,0:T(8,128)}, u32[]{:S(2)}) copy-start(f32[128,128]{1,0:T(8,128)} %param.12) | copy-start | bytes 196612
  0.7 47.9 %copy-start.7 = (s32[1,64]{1,0:T(1,128)S(1)}, s32[1,64]{1,0:T(1,128)}, u32[]{:S(2)}) copy-start(s32[1,64]{1,0:T(1,128)} %param.13) | copy-start | bytes 772
  1.5 5.9 %collective-permute-start.1 = (f32[2,1,128]{2,1,0:T(1,128)S(1)}, f32[2,1,128]{2,1,0:T(1,128)S(1)}, u32[]{:S(2)}, u32[]{:S(2)}) collective-permute-start(f32[2,1,128]{2,1,0:T(1,128)S(1)} %get-tuple-element.7), channel_id=1, source_target_pairs={{16,0},{32,16},{48,32},{64,48},{80,64},{96,80},{112,96},{128,112},... | collective-permute-start | bytes 3080 | tf_op jit(solution)/shard_map/ppermute | solution.py:20
  5.5 9.7 %collective-permute-start = (f32[2,1,128]{2,1,0:T(1,128)S(1)}, f32[2,1,128]{2,1,0:T(1,128)S(1)}, u32[]{:S(2)}, u32[]{:S(2)}) collective-permute-start(f32[2,1,128]{2,1,0:T(1,128)S(1)} %get-tuple-element.6), channel_id=1, source_target_pairs={{0,16},{16,32},{32,48},{48,64},{64,80},{80,96},{96,112},{112,128},... | collective-permute-start | bytes 3080 | tf_op jit(solution)/shard_map/ppermute | solution.py:19
  16.2 4.3 %collective-permute-start.3 = (f32[2,130,1]{2,1,0:T(8,128)S(1)}, f32[2,130,1]{2,1,0:T(8,128)S(1)}, u32[]{:S(2)}, u32[]{:S(2)}) collective-permute-start(f32[2,130,1]{2,1,0:T(8,128)S(1)} %get-tuple-element.5), channel_id=1, source_target_pairs={{1,0},{2,1},{3,2},{4,3},{5,4},{6,5},{7,6},{8,7},{9,8},{10,9},{11,1... | collective-permute-start | bytes 3128 | tf_op jit(solution)/shard_map/ppermute | solution.py:20
  17.5 4.0 %collective-permute-start.2 = (f32[2,130,1]{2,1,0:T(8,128)S(1)}, f32[2,130,1]{2,1,0:T(8,128)S(1)}, u32[]{:S(2)}, u32[]{:S(2)}) collective-permute-start(f32[2,130,1]{2,1,0:T(8,128)S(1)} %get-tuple-element.4), channel_id=1, source_target_pairs={{0,1},{1,2},{2,3},{3,4},{4,5},{5,6},{6,7},{7,8},{8,9},{9,10},{10,1... | collective-permute-start | bytes 3128 | tf_op jit(solution)/shard_map/ppermute | solution.py:19
  23.7 5.9 %collective-permute-start.5 = (f32[1,128]{1,0:T(1,128)S(1)}, f32[1,128]{1,0:T(1,128)S(1)}, u32[]{:S(2)}, u32[]{:S(2)}) collective-permute-start(f32[1,128]{1,0:T(1,128)S(1)} %get-tuple-element.15), channel_id=1, source_target_pairs={{16,0},{32,16},{48,32},{64,48},{80,64},{96,80},{112,96},{128,112},... | collective-permute-start | bytes 1544 | tf_op jit(solution)/shard_map/ppermute | solution.py:20
  25.6 9.7 %collective-permute-start.4 = (f32[1,128]{1,0:T(1,128)S(1)}, f32[1,128]{1,0:T(1,128)S(1)}, u32[]{:S(2)}, u32[]{:S(2)}) collective-permute-start(f32[1,128]{1,0:T(1,128)S(1)} %get-tuple-element.14), channel_id=1, source_target_pairs={{0,16},{16,32},{32,48},{48,64},{64,80},{80,96},{96,112},{112,128},... | collective-permute-start | bytes 1544 | tf_op jit(solution)/shard_map/ppermute | solution.py:19
  35.4 5.3 %collective-permute-start.7 = (f32[130,1]{1,0:T(8,128)S(1)}, f32[130,1]{1,0:T(8,128)S(1)}, u32[]{:S(2)}, u32[]{:S(2)}) collective-permute-start(f32[130,1]{1,0:T(8,128)S(1)} %get-tuple-element.11), channel_id=1, source_target_pairs={{1,0},{2,1},{3,2},{4,3},{5,4},{6,5},{7,6},{8,7},{9,8},{10,9},{11,1... | collective-permute-start | bytes 1568 | tf_op jit(solution)/shard_map/ppermute | solution.py:20
  36.7 4.8 %collective-permute-start.6 = (f32[130,1]{1,0:T(8,128)S(1)}, f32[130,1]{1,0:T(8,128)S(1)}, u32[]{:S(2)}, u32[]{:S(2)}) collective-permute-start(f32[130,1]{1,0:T(8,128)S(1)} %get-tuple-element.10), channel_id=1, source_target_pairs={{0,1},{1,2},{2,3},{3,4},{4,5},{5,6},{6,7},{7,8},{8,9},{9,10},{10,1... | collective-permute-start | bytes 1568 | tf_op jit(solution)/shard_map/ppermute | solution.py:19
  42.7 5.9 %collective-permute-start.9 = (f32[1,128]{1,0:T(1,128)S(1)}, f32[1,128]{1,0:T(1,128)S(1)}, u32[]{:S(2)}, u32[]{:S(2)}) collective-permute-start(f32[1,128]{1,0:T(1,128)S(1)} %get-tuple-element.13), channel_id=1, source_target_pairs={{16,0},{32,16},{48,32},{64,48},{80,64},{96,80},{112,96},{128,112},... | collective-permute-start | bytes 1544 | tf_op jit(solution)/shard_map/ppermute | solution.py:20
  44.7 9.7 %collective-permute-start.8 = (f32[1,128]{1,0:T(1,128)S(1)}, f32[1,128]{1,0:T(1,128)S(1)}, u32[]{:S(2)}, u32[]{:S(2)}) collective-permute-start(f32[1,128]{1,0:T(1,128)S(1)} %get-tuple-element.12), channel_id=1, source_target_pairs={{0,16},{16,32},{32,48},{48,64},{64,80},{80,96},{96,112},{112,128},... | collective-permute-start | bytes 1544 | tf_op jit(solution)/shard_map/ppermute | solution.py:19
  48.6 27.6 %copy-start.4 = (s32[1,64,4]{1,2,0:T(4,128)S(1)}, s32[1,64,4]{1,2,0:T(4,128)}, u32[]{:S(2)}) copy-start(s32[1,64,4]{1,2,0:T(4,128)} %param.16) | copy-start | bytes 3076
  48.6 27.6 %copy-start.5 = (s32[1,64,4]{1,2,0:T(4,128)S(1)}, s32[1,64,4]{1,2,0:T(4,128)}, u32[]{:S(2)}) copy-start(s32[1,64,4]{1,2,0:T(4,128)} %param.15) | copy-start | bytes 3076
  54.4 22.1 %copy-start.6 = (s32[1,64,4]{1,2,0:T(4,128)S(1)}, s32[1,64,4]{1,2,0:T(4,128)}, u32[]{:S(2)}) copy-start(s32[1,64,4]{1,2,0:T(4,128)} %param.17) | copy-start | bytes 3076
  54.5 7.1 %collective-permute-start.11 = (f32[130,1]{1,0:T(8,128)S(1)}, f32[130,1]{1,0:T(8,128)S(1)}, u32[]{:S(2)}, u32[]{:S(2)}) collective-permute-start(f32[130,1]{1,0:T(8,128)S(1)} %get-tuple-element.9), channel_id=1, source_target_pairs={{1,0},{2,1},{3,2},{4,3},{5,4},{6,5},{7,6},{8,7},{9,8},{10,9},{11,1... | collective-permute-start | bytes 1568 | tf_op jit(solution)/shard_map/ppermute | solution.py:20
  55.8 6.3 %collective-permute-start.10 = (f32[130,1]{1,0:T(8,128)S(1)}, f32[130,1]{1,0:T(8,128)S(1)}, u32[]{:S(2)}, u32[]{:S(2)}) collective-permute-start(f32[130,1]{1,0:T(8,128)S(1)} %get-tuple-element.8), channel_id=1, source_target_pairs={{0,1},{1,2},{2,3},{3,4},{4,5},{5,6},{6,7},{7,8},{8,9},{9,10},{10,1... | collective-permute-start | bytes 1568 | tf_op jit(solution)/shard_map/ppermute | solution.py:19
  64.8 28.0 %all-to-all-start = ((f32[16,64,256]{2,1,0:T(8,128)}), f32[16,64,256]{2,1,0:T(8,128)S(1)}, u32[]{:S(2)}, u32[]{:S(2)}) async-start(f32[16,64,256]{2,1,0:T(8,128)} %stack.11), calls=%async_computation | async-start | bytes 2097152 | tf_op jit(solution)/shard_map/all_to_all | solution.py:86
  94.1 6.0 %copy-start.1 = (f32[1,64,4,16,256]{4,3,2,1,0:T(8,128)S(1)}, f32[1,64,4,16,256]{4,3,2,1,0:T(8,128)}, u32[]{:S(2)}) copy-start(f32[1,64,4,16,256]{4,3,2,1,0:T(8,128)} %param.18) | copy-start | bytes 12582916
